TPU v7x, 512 devices: a whole 4x8x8 slice. The times are simulated.
512 devices in a mesh: cfg: 2 (over core), pipe: 4 (over x), seq: 64 (over y, z).
Axes of the slice: x: 4, y: 8, z: 8, core: 2. Of those that a mesh axis runs over, the one named last changes fastest.
Arguments:
- latent: bfloat16 [4, 512, 2048], P(None, 'seq'), may hold values from -6 to 6
- modulation: float32 [4, 2, 3, 2048], P('pipe', 'cfg'), may hold values from -4 to 4
- qkv_weight: bfloat16 [4, 2048, 6144], P('pipe', None, 'seq'), may hold values from -0.125 to 0.125
- out_weight: bfloat16 [4, 2048, 2048], P('pipe', 'seq'), may hold values from -0.125 to 0.125
- norm_gain: float32 [4, 2, 128], P('pipe'), may hold values from 1.2 to 2
- stale_kv: bfloat16 [4, 2, 2, 4, 64, 8, 8, 256], P('pipe', 'cfg', None, None, 'seq'), may hold values from -2 to 2
Outputs:
- guided: bfloat16 [4, 512, 2048], P('pipe', 'seq', 'cfg')
- next_kv: bfloat16 [4, 2, 2, 4, 64, 8, 8, 256], P('pipe', 'cfg', None, None, 'seq')
All inputs are finite; a program needn't handle non-finite values.
Results may differ from a plain program's by a relative error of at most 0.033.
Values may be sent and summed in bfloat16 or wider, within the bound.
A program may use at most 64 MiB of HBM per device.

v0:
```python
import math

import jax
import jax.numpy as jnp
from jax import lax
from jax.sharding import PartitionSpec as P

GUIDANCE_SCALE = 6.0
EPSILON = 1e-06


def swapped(value, axis, bit):
    return lax.ppermute(value, axis, [(i, i ^ 1 << bit) for i in range(lax.axis_size(axis))])


def from_behind(value, axis, steps):
    count = lax.axis_size(axis)
    initial, last = (max(0, -steps), min(count, count - steps))
    return lax.ppermute(value, axis, [(source, source + steps) for source in range(initial, last)])


def spread_2(value, axis, root):
    mine = lax.axis_index(axis) == root
    return lax.psum(jnp.where(mine, value, jnp.zeros_like(value)), axis)


def layer_norm(values):
    center = values - jnp.mean(values, axis=-1, keepdims=True)
    spread = jnp.mean(center * center, axis=-1, keepdims=True)
    return center * lax.rsqrt(spread + EPSILON)


def head_norm(values, gain_row):
    return (
        values * lax.rsqrt(jnp.mean(values * values, axis=-1, keepdims=True) + EPSILON) * gain_row
    )


def join_pair(is_upper, mine, theirs, axis_dim):
    return jnp.where(
        is_upper,
        jnp.concatenate((theirs, mine), axis_dim),
        jnp.concatenate((mine, theirs), axis_dim),
    )


def local(latent, modulation, qkv_weight, out_weight, norm_gain, stale_kv):
    seq_count = lax.axis_size("seq")
    seq_rank = lax.axis_index("seq")
    section_count = lax.axis_size("pipe")
    section_rank = lax.axis_index("pipe")
    branch_rank = lax.axis_index("cfg")
    patches, tok_dev, model_width = latent.shape
    head_dim = norm_gain.shape[2]
    slice_count = min(seq_count, 8)
    member_count = seq_count // slice_count
    member_bits = member_count.bit_length() - 1
    slice_bits = slice_count.bit_length() - 1
    own_member = seq_rank % member_count
    own_slice = seq_rank // member_count
    local_width = stale_kv.shape[7]
    local_heads = local_width // head_dim
    group_rows = slice_count * tok_dev
    divisor = math.sqrt(head_dim)
    shift_row = modulation[0, 0, 0]
    scale_row = modulation[0, 0, 1]
    gate_row = modulation[0, 0, 2]
    query_gain = norm_gain[0, 0]
    key_gain = norm_gain[0, 1]
    own_cache = stale_kv[0, 0].reshape(2, patches, group_rows, local_width)
    qkv_piece = qkv_weight[0]
    out_piece = out_weight[0]
    group_cache = own_cache[None]
    qkv_slice = qkv_piece
    out_slice = out_piece
    for level_index in range(member_bits):
        got_qkv, got_out, got_cache = swapped(
            (qkv_slice, out_slice, group_cache), "seq", level_index
        )
        is_upper = own_member >> level_index & 1 == 1
        qkv_slice = join_pair(is_upper, qkv_slice, got_qkv, 1)
        out_slice = join_pair(is_upper, out_slice, got_out, 0)
        group_cache = join_pair(is_upper, group_cache, got_cache, 0)

    def tick(tick_index, carried):
        incoming, own_cache, results = carried
        patch_index = tick_index - section_rank
        is_active = jnp.logical_and(patch_index >= 0, patch_index < patches)
        patch_slot = jnp.clip(patch_index, 0, patches - 1)
        first_input = lax.dynamic_index_in_dim(latent, patch_slot, 0, keepdims=False)
        hidden_in = jnp.where(section_rank == 0, first_input, incoming)
        normed = layer_norm(hidden_in.astype(jnp.float32))
        group_features = (normed * (1.0 + scale_row) + shift_row).astype(jnp.bfloat16)
        for level_index in range(slice_bits):
            got_rows = swapped(group_features, "seq", member_bits + level_index)
            is_upper = own_slice >> level_index & 1 == 1
            group_features = join_pair(is_upper, group_features, got_rows, 0)
        mixed = jnp.dot(group_features, qkv_slice, preferred_element_type=jnp.float32)
        mixed = mixed.reshape(group_rows, local_heads, 3, head_dim)
        queries = head_norm(mixed[:, :, 0], query_gain).astype(jnp.bfloat16)
        fresh_rows = jnp.stack((head_norm(mixed[:, :, 1], key_gain), mixed[:, :, 2])).astype(
            jnp.bfloat16
        )
        updated = lax.dynamic_update_index_in_dim(
            own_cache, fresh_rows.reshape(2, group_rows, local_width), patch_slot, 1
        )

        def compute():
            view = lax.dynamic_update_index_in_dim(group_cache, updated, own_member, 0)
            key_rows = view[:, 0].reshape(-1, local_heads, head_dim)
            value_rows = view[:, 1].reshape(-1, local_heads, head_dim)
            scores = (
                jnp.einsum("qhd,khd->hqk", queries, key_rows, preferred_element_type=jnp.float32)
                / divisor
            )
            weights = jnp.exp(scores)
            weight_total = jnp.sum(weights, axis=-1)
            summed = jnp.einsum(
                "hqk,khd->qhd",
                weights.astype(jnp.bfloat16),
                value_rows,
                preferred_element_type=jnp.float32,
            )
            return (
                (summed / weight_total.T[:, :, None])
                .astype(jnp.bfloat16)
                .reshape(group_rows, local_width)
            )

        attended = lax.cond(
            is_active, compute, lambda: jnp.zeros((group_rows, local_width), jnp.bfloat16)
        )
        partial_out = jnp.dot(attended, out_slice, preferred_element_type=jnp.float32)
        for level_index in reversed(range(slice_bits)):
            half_rows = partial_out.shape[0] // 2
            is_upper = own_slice >> level_index & 1 == 1
            keep_rows = jnp.where(is_upper, partial_out[half_rows:], partial_out[:half_rows])
            send_rows = jnp.where(is_upper, partial_out[:half_rows], partial_out[half_rows:])
            partial_out = keep_rows + swapped(
                send_rows.astype(jnp.bfloat16), "seq", member_bits + level_index
            ).astype(send_rows.dtype)
        hidden_out = (hidden_in.astype(jnp.float32) + gate_row * partial_out).astype(jnp.bfloat16)
        own_cache = jnp.where(is_active, updated, own_cache)
        results = jnp.where(
            is_active, lax.dynamic_update_index_in_dim(results, hidden_out, patch_slot, 0), results
        )
        incoming = from_behind(hidden_out, "pipe", 1)
        return (incoming, own_cache, results)

    initial = (
        jnp.zeros((tok_dev, model_width), jnp.bfloat16),
        own_cache,
        jnp.zeros((patches, tok_dev, model_width), jnp.bfloat16),
    )
    incoming, own_cache, results = lax.fori_loop(0, patches + section_count - 1, tick, initial)
    half_width = model_width // 2
    partner_out = swapped(results, "cfg", 0)
    own_half = lax.dynamic_slice_in_dim(results, branch_rank * half_width, half_width, 2).astype(
        jnp.float32
    )
    partner_half = lax.dynamic_slice_in_dim(
        partner_out, branch_rank * half_width, half_width, 2
    ).astype(jnp.float32)
    conditional = jnp.where(branch_rank == 0, own_half, partner_half)
    unconditional = jnp.where(branch_rank == 0, partner_half, own_half)
    guided = (unconditional + GUIDANCE_SCALE * (conditional - unconditional)).astype(jnp.bfloat16)
    spread_all = spread_2(guided, "pipe", section_count - 1)
    per_section = patches // section_count
    guided_out = lax.dynamic_slice_in_dim(spread_all, section_rank * per_section, per_section, 0)
    next_cache = own_cache.reshape(stale_kv.shape)
    return (guided_out, next_cache)


def solution(mesh):
    placed = (
        P(None, "seq", None),
        P("pipe", "cfg", None, None),
        P("pipe", None, "seq"),
        P("pipe", "seq", None),
        P("pipe", None, None),
        P("pipe", "cfg", None, None, "seq", None, None, None),
    )
    return jax.shard_map(
        local,
        mesh=mesh,
        in_specs=placed,
        out_specs=(P("pipe", "seq", "cfg"), P("pipe", "cfg", None, None, "seq", None, None, None)),
        check_vma=False,
    )
```

profile of v0, /device:TPU:32, one launch (start us, length us, event | category | flops | bytes accessed | tf_op | source)
XLA Modules:
  0.0 968.2 jit_solution(14292105053451538449)
XLA Ops:
  13.2 9.3 collective-permute-done.7
  23.8 6.1 collective-permute-start.8
  35.8 17.5 %collective-permute-done.10 = bf16[1,2,4,64,256]{4,3,2,0,1:T(8,128)(2,1)S(1)} collective-permute-done((bf16[1,2,4,64,256]{4,3,2,0,1:T(8,128)(2,1)}, bf16[1,2,4,64,256]{4,3,2,0,1:T(8,128)(2,1)S(1)}, u32[]{:S(2)}, u32[]{:S(2)}) %collective-permute-start.10) | collective-permute-done | bytes 262176 | tf_op jit(solution)/shard_map/ppermute | solution.py:13
  61.3 20.4 %collective-permute-done.8 = bf16[2048,192]{0,1:T(8,128)(2,1)S(1)} collective-permute-done((bf16[2048,192]{0,1:T(8,128)(2,1)S(1)}, bf16[2048,192]{0,1:T(8,128)(2,1)S(1)}, u32[]{:S(2)}, u32[]{:S(2)}) %collective-permute-start.8) | collective-permute-done | bytes 786464 | tf_op jit(solution)/shard_map/ppermute | solution.py:13
  82.2 8.5 collective-permute-start.9
  93.1 42.4 %collective-permute-start.12 = (bf16[4,2,4,64,256]{4,3,2,0,1:T(8,128)(2,1)S(1)}, bf16[4,2,4,64,256]{4,3,2,0,1:T(8,128)(2,1)}, u32[]{:S(2)}, u32[]{:S(2)}) collective-permute-start(bf16[4,2,4,64,256]{4,3,2,0,1:T(8,128)(2,1)S(1)} %maximum_select_fusion.7), channel_id=1, source_target_pairs={{0,4},{1,5},{2,6},{3,7},{4,0},{5,1},{6,2},{7,3},{8,12},{9,13},{10,... | collective-permute-start | bytes 3145736 | tf_op jit(solution)/shard_map/ppermute | solution.py:13
  135.6 82.8 %collective-permute-start.15 = (bf16[128,2048]{1,0:T(8,128)(2,1)S(1)}, bf16[128,2048]{1,0:T(8,128)(2,1)}, u32[]{:S(2)}, u32[]{:S(2)}) collective-permute-start(bf16[128,2048]{1,0:T(8,128)(2,1)S(1)} %maximum_select_fusion.11), channel_id=1, source_target_pairs={{0,4},{1,5},{2,6},{3,7},{4,0},{5,1},{6,2},{7,3},{8,12},{9,13},{10,... | collective-permute-start | bytes 1572872 | tf_op jit(solution)/shard_map/ppermute | solution.py:13
  219.6 18.4 %collective-permute-done.15 = bf16[128,2048]{1,0:T(8,128)(2,1)} collective-permute-done((bf16[128,2048]{1,0:T(8,128)(2,1)S(1)}, bf16[128,2048]{1,0:T(8,128)(2,1)}, u32[]{:S(2)}, u32[]{:S(2)}) %collective-permute-start.15) | collective-permute-done | bytes 524320 | tf_op jit(solution)/shard_map/ppermute | solution.py:13
  252.4 607.8 %while.19 = (s32[]{:T(128)}, bf16[8,2048]{1,0:T(8,128)(2,1)}, bf16[2,4,64,256]{3,2,1,0:T(8,128)(2,1)}, bf16[4,8,2048]{2,1,0:T(8,128)(2,1)}, pred[]{:T(512)}, /*i...) while((s32[]{:T(128)}, bf16[8,2048]{1,0:T(8,128)(2,1)}, ...), condition=%wide.region_8.9_spmd, body=%wide.region_0.8_spmd.sunk | while | flops 406718592 | bytes 29705688 | solution.py:155
  271.5 8.7 collective-permute-done.2
  295.6 11.6 %conditional.2 = (bf16[64,256]{1,0:T(8,128)(2,1)S(1)}) conditional(s32[]{:T(128)} %convert_element_type.212, () %tuple.70, (bf16[2,4,64,256]{3,2,1,0:T(8,128)(2,1)S(1)}, s32[]{:T(128)}, bf16[8,2,4,64,256]{4,3,2,0,1:T(8,128)(2,1)}, bf16[64,2,128]{2,1,0:T(2,128)(2,1)}) %tuple.71), branch_computations={%region_5.5_spmd, %region_6.7_spmd} | conditional | flops 135036800 | bytes 16516170 | solution.py:130
  310.8 11.3 %collective-permute-done.3 = bf16[32,2048]{1,0:T(8,128)(2,1)S(1)} collective-permute-done((bf16[32,2048]{1,0:T(8,128)(2,1)S(1)}, bf16[32,2048]{1,0:T(8,128)(2,1)S(1)}, u32[]{:S(2)}, u32[]{:S(2)}) %collective-permute-start.3) | collective-permute-done | bytes 131104 | tf_op jit(solution)/shard_map/while/body/eval_jaxpr/ppermute | solution.py:13
  358.8 8.1 collective-permute-done.2
  382.3 11.6 %conditional.2 = (bf16[64,256]{1,0:T(8,128)(2,1)S(1)}) conditional(s32[]{:T(128)} %convert_element_type.212, () %tuple.70, (bf16[2,4,64,256]{3,2,1,0:T(8,128)(2,1)S(1)}, s32[]{:T(128)}, bf16[8,2,4,64,256]{4,3,2,0,1:T(8,128)(2,1)}, bf16[64,2,128]{2,1,0:T(2,128)(2,1)}) %tuple.71), branch_computations={%region_5.5_spmd, %region_6.7_spmd} | conditional | flops 135036800 | bytes 16516170 | solution.py:130
  397.5 9.7 %collective-permute-done.3 = bf16[32,2048]{1,0:T(8,128)(2,1)S(1)} collective-permute-done((bf16[32,2048]{1,0:T(8,128)(2,1)S(1)}, bf16[32,2048]{1,0:T(8,128)(2,1)S(1)}, u32[]{:S(2)}, u32[]{:S(2)}) %collective-permute-start.3) | collective-permute-done | bytes 131104 | tf_op jit(solution)/shard_map/while/body/eval_jaxpr/ppermute | solution.py:13
  449.3 7.2 collective-permute-done.2
  471.9 11.6 %conditional.2 = (bf16[64,256]{1,0:T(8,128)(2,1)S(1)}) conditional(s32[]{:T(128)} %convert_element_type.212, () %tuple.70, (bf16[2,4,64,256]{3,2,1,0:T(8,128)(2,1)S(1)}, s32[]{:T(128)}, bf16[8,2,4,64,256]{4,3,2,0,1:T(8,128)(2,1)}, bf16[64,2,128]{2,1,0:T(2,128)(2,1)}) %tuple.71), branch_computations={%region_5.5_spmd, %region_6.7_spmd} | conditional | flops 135036800 | bytes 16516170 | solution.py:130
  487.5 8.4 collective-permute-done.3
  511.6 6.2 collective-permute-start.6
  537.8 7.2 collective-permute-done.2
  560.4 11.6 %conditional.2 = (bf16[64,256]{1,0:T(8,128)(2,1)S(1)}) conditional(s32[]{:T(128)} %convert_element_type.212, () %tuple.70, (bf16[2,4,64,256]{3,2,1,0:T(8,128)(2,1)S(1)}, s32[]{:T(128)}, bf16[8,2,4,64,256]{4,3,2,0,1:T(8,128)(2,1)}, bf16[64,2,128]{2,1,0:T(2,128)(2,1)}) %tuple.71), branch_computations={%region_5.5_spmd, %region_6.7_spmd} | conditional | flops 135036800 | bytes 16516170 | solution.py:130
  576.1 8.4 collective-permute-done.3
  586.5 7.2 collective-permute-done.4
  625.7 6.7 collective-permute-done.2
  652.4 7.8 collective-permute-done.3
  675.5 17.1 %collective-permute-start.6 = (bf16[8,2048]{1,0:T(8,128)(2,1)S(1)}, bf16[8,2048]{1,0:T(8,128)(2,1)}, u32[]{:S(2)}, u32[]{:S(2)}) collective-permute-start(bf16[8,2048]{1,0:T(8,128)(2,1)S(1)} %get-tuple-element.663), channel_id=1, source_target_pairs={{0,64},{64,128},{128,192},{1,65},{65,129},{129,193},{2,66},{66,130... | collective-permute-start | bytes 98312 | tf_op jit(solution)/shard_map/while/body/eval_jaxpr/ppermute | solution.py:19
  715.6 7.9 collective-permute-done.2
  744.9 8.2 collective-permute-done.3
  792.8 9.0 collective-permute-done.2
  820.8 10.2 %collective-permute-done.3 = bf16[32,2048]{1,0:T(8,128)(2,1)S(1)} collective-permute-done((bf16[32,2048]{1,0:T(8,128)(2,1)S(1)}, bf16[32,2048]{1,0:T(8,128)(2,1)S(1)}, u32[]{:S(2)}, u32[]{:S(2)}) %collective-permute-start.3) | collective-permute-done | bytes 131104 | tf_op jit(solution)/shard_map/while/body/eval_jaxpr/ppermute | solution.py:13
  846.3 12.3 %collective-permute-start.6 = (bf16[8,2048]{1,0:T(8,128)(2,1)S(1)}, bf16[8,2048]{1,0:T(8,128)(2,1)}, u32[]{:S(2)}, u32[]{:S(2)}) collective-permute-start(bf16[8,2048]{1,0:T(8,128)(2,1)S(1)} %get-tuple-element.663), channel_id=1, source_target_pairs={{0,64},{64,128},{128,192},{1,65},{65,129},{129,193},{2,66},{66,130... | collective-permute-start | bytes 98312 | tf_op jit(solution)/shard_map/while/body/eval_jaxpr/ppermute | solution.py:19
  865.2 94.8 %all-reduce.2.cloned.1.call-done = bf16[4,8,1024]{2,1,0:T(8,128)(2,1)} async-done(((bf16[4,8,1024]{2,1,0:T(8,128)(2,1)}), bf16[4,8,1024]{2,1,0:T(8,128)(2,1)}) %all-reduce.2.cloned.1.call-update) | async-done | bytes 65552 | tf_op jit(solution)/shard_map/psum | solution.py:24
  (401 shorter events, 491.0 us)
Async XLA Ops:
  7.2 952.8 %all-reduce.2.cloned.1.call-start = ((), (), s32[]{:S(2)}) async-start(), calls=%async_computation | async-start | bytes 131072 | tf_op jit(solution)/shard_map/psum | solution.py:24
  8.9 13.6 %collective-permute-start.7 = (bf16[2048,96]{0,1:T(8,128)(2,1)}, bf16[2048,96]{0,1:T(8,128)(2,1)S(1)}, u32[]{:S(2)}, u32[]{:S(2)}) collective-permute-start(bf16[2048,96]{0,1:T(8,128)(2,1)} %bitcast.81), channel_id=1, source_target_pairs={{0,1},{1,0},{2,3},{3,2},{4,5},{5,4},{6,7},{7,6},{8,9},{9,8},{10,11... | collective-permute-start | bytes 1179656 | tf_op jit(solution)/shard_map/ppermute | solution.py:13
  23.8 57.8 %collective-permute-start.8 = (bf16[2048,192]{0,1:T(8,128)(2,1)S(1)}, bf16[2048,192]{0,1:T(8,128)(2,1)S(1)}, u32[]{:S(2)}, u32[]{:S(2)}) collective-permute-start(bf16[2048,192]{0,1:T(8,128)(2,1)S(1)} %maximum_select_fusion.9), channel_id=1, source_target_pairs={{0,2},{1,3},{2,0},{3,1},{4,6},{5,7},{6,4},{7,5},{8,10},{9,11},{10,... | collective-permute-start | bytes 2359304 | tf_op jit(solution)/shard_map/ppermute | solution.py:13
  29.9 23.4 %collective-permute-start.10 = (bf16[1,2,4,64,256]{4,3,2,0,1:T(8,128)(2,1)}, bf16[1,2,4,64,256]{4,3,2,0,1:T(8,128)(2,1)S(1)}, u32[]{:S(2)}, u32[]{:S(2)}) collective-permute-start(bf16[1,2,4,64,256]{4,3,2,0,1:T(8,128)(2,1)} %bitcast.16), channel_id=1, source_target_pairs={{0,1},{1,0},{2,3},{3,2},{4,5},{5,4},{6,7},{7,6},{8,9},{9,8},{10,11... | collective-permute-start | bytes 786440 | tf_op jit(solution)/shard_map/ppermute | solution.py:13
  33.6 24.8 %collective-permute-start.13 = (bf16[32,2048]{1,0:T(8,128)(2,1)S(1)}, bf16[32,2048]{1,0:T(8,128)(2,1)S(1)}, u32[]{:S(2)}, u32[]{:S(2)}) collective-permute-start(bf16[32,2048]{1,0:T(8,128)(2,1)S(1)} %bitcast.85), channel_id=1, source_target_pairs={{0,1},{1,0},{2,3},{3,2},{4,5},{5,4},{6,7},{7,6},{8,9},{9,8},{10,11... | collective-permute-start | bytes 393224 | tf_op jit(solution)/shard_map/ppermute | solution.py:13
  54.4 38.5 %collective-permute-start.11 = (bf16[2,2,4,64,256]{4,3,2,0,1:T(8,128)(2,1)S(1)}, bf16[2,2,4,64,256]{4,3,2,0,1:T(8,128)(2,1)S(1)}, u32[]{:S(2)}, u32[]{:S(2)}) collective-permute-start(bf16[2,2,4,64,256]{4,3,2,0,1:T(8,128)(2,1)S(1)} %maximum_select_fusion.10), channel_id=1, source_target_pairs={{0,2},{1,3},{2,0},{3,1},{4,6},{5,7},{6,4},{7,5},{8,10},{9,11},{10,... | collective-permute-start | bytes 1572872 | tf_op jit(solution)/shard_map/ppermute | solution.py:13
  58.5 77.0 %collective-permute-start.14 = (bf16[64,2048]{1,0:T(8,128)(2,1)S(1)}, bf16[64,2048]{1,0:T(8,128)(2,1)S(1)}, u32[]{:S(2)}, u32[]{:S(2)}) collective-permute-start(bf16[64,2048]{1,0:T(8,128)(2,1)S(1)} %maximum_select_fusion.12), channel_id=1, source_target_pairs={{0,2},{1,3},{2,0},{3,1},{4,6},{5,7},{6,4},{7,5},{8,10},{9,11},{10,... | collective-permute-start | bytes 786440 | tf_op jit(solution)/shard_map/ppermute | solution.py:13
  82.2 161.5 %collective-permute-start.9 = (bf16[2048,384]{0,1:T(8,128)(2,1)S(1)}, bf16[2048,384]{0,1:T(8,128)(2,1)}, u32[]{:S(2)}, u32[]{:S(2)}) collective-permute-start(bf16[2048,384]{0,1:T(8,128)(2,1)S(1)} %maximum_select_fusion.6), channel_id=1, source_target_pairs={{0,4},{1,5},{2,6},{3,7},{4,0},{5,1},{6,2},{7,3},{8,12},{9,13},{10,... | collective-permute-start | bytes 4718600 | tf_op jit(solution)/shard_map/ppermute | solution.py:13
  93.1 147.4 %collective-permute-start.12 = (bf16[4,2,4,64,256]{4,3,2,0,1:T(8,128)(2,1)S(1)}, bf16[4,2,4,64,256]{4,3,2,0,1:T(8,128)(2,1)}, u32[]{:S(2)}, u32[]{:S(2)}) collective-permute-start(bf16[4,2,4,64,256]{4,3,2,0,1:T(8,128)(2,1)S(1)} %maximum_select_fusion.7), channel_id=1, source_target_pairs={{0,4},{1,5},{2,6},{3,7},{4,0},{5,1},{6,2},{7,3},{8,12},{9,13},{10,... | collective-permute-start | bytes 3145736 | tf_op jit(solution)/shard_map/ppermute | solution.py:13
  135.6 102.4 %collective-permute-start.15 = (bf16[128,2048]{1,0:T(8,128)(2,1)S(1)}, bf16[128,2048]{1,0:T(8,128)(2,1)}, u32[]{:S(2)}, u32[]{:S(2)}) collective-permute-start(bf16[128,2048]{1,0:T(8,128)(2,1)S(1)} %maximum_select_fusion.11), channel_id=1, source_target_pairs={{0,4},{1,5},{2,6},{3,7},{4,0},{5,1},{6,2},{7,3},{8,12},{9,13},{10,... | collective-permute-start | bytes 1572872 | tf_op jit(solution)/shard_map/ppermute | solution.py:13
  260.5 7.8 collective-permute-start.1
  268.3 11.9 %collective-permute-start.2 = (bf16[32,2048]{1,0:T(8,128)(2,1)S(1)}, bf16[32,2048]{1,0:T(8,128)(2,1)S(1)}, u32[]{:S(2)}, u32[]{:S(2)}) collective-permute-start(bf16[32,2048]{1,0:T(8,128)(2,1)S(1)} %maximum_select_fusion.18), channel_id=1, source_target_pairs={{0,32},{1,33},{2,34},{3,35},{4,36},{5,37},{6,38},{7,39},{8,40},{9,... | collective-permute-start | bytes 393224 | tf_op jit(solution)/shard_map/while/body/eval_jaxpr/ppermute | solution.py:13
  308.8 13.2 %collective-permute-start.3 = (bf16[32,2048]{1,0:T(8,128)(2,1)S(1)}, bf16[32,2048]{1,0:T(8,128)(2,1)S(1)}, u32[]{:S(2)}, u32[]{:S(2)}) collective-permute-start(bf16[32,2048]{1,0:T(8,128)(2,1)S(1)} %select_convert_fusion.6), channel_id=1, source_target_pairs={{0,32},{1,33},{2,34},{3,35},{4,36},{5,37},{6,38},{7,39},{8,40},{9,... | collective-permute-start | bytes 393224 | tf_op jit(solution)/shard_map/while/body/eval_jaxpr/ppermute | solution.py:13
  348.3 7.3 collective-permute-start.1
  355.7 11.3 %collective-permute-start.2 = (bf16[32,2048]{1,0:T(8,128)(2,1)S(1)}, bf16[32,2048]{1,0:T(8,128)(2,1)S(1)}, u32[]{:S(2)}, u32[]{:S(2)}) collective-permute-start(bf16[32,2048]{1,0:T(8,128)(2,1)S(1)} %maximum_select_fusion.18), channel_id=1, source_target_pairs={{0,32},{1,33},{2,34},{3,35},{4,36},{5,37},{6,38},{7,39},{8,40},{9,... | collective-permute-start | bytes 393224 | tf_op jit(solution)/shard_map/while/body/eval_jaxpr/ppermute | solution.py:13
  395.5 11.6 %collective-permute-start.3 = (bf16[32,2048]{1,0:T(8,128)(2,1)S(1)}, bf16[32,2048]{1,0:T(8,128)(2,1)S(1)}, u32[]{:S(2)}, u32[]{:S(2)}) collective-permute-start(bf16[32,2048]{1,0:T(8,128)(2,1)S(1)} %select_convert_fusion.6), channel_id=1, source_target_pairs={{0,32},{1,33},{2,34},{3,35},{4,36},{5,37},{6,38},{7,39},{8,40},{9,... | collective-permute-start | bytes 393224 | tf_op jit(solution)/shard_map/while/body/eval_jaxpr/ppermute | solution.py:13
  407.2 7.8 collective-permute-start.4
  444.5 12.0 %collective-permute-start.2 = (bf16[32,2048]{1,0:T(8,128)(2,1)S(1)}, bf16[32,2048]{1,0:T(8,128)(2,1)S(1)}, u32[]{:S(2)}, u32[]{:S(2)}) collective-permute-start(bf16[32,2048]{1,0:T(8,128)(2,1)S(1)} %maximum_select_fusion.18), channel_id=1, source_target_pairs={{0,32},{1,33},{2,34},{3,35},{4,36},{5,37},{6,38},{7,39},{8,40},{9,... | collective-permute-start | bytes 393224 | tf_op jit(solution)/shard_map/while/body/eval_jaxpr/ppermute | solution.py:13
  485.1 10.9 %collective-permute-start.3 = (bf16[32,2048]{1,0:T(8,128)(2,1)S(1)}, bf16[32,2048]{1,0:T(8,128)(2,1)S(1)}, u32[]{:S(2)}, u32[]{:S(2)}) collective-permute-start(bf16[32,2048]{1,0:T(8,128)(2,1)S(1)} %select_convert_fusion.6), channel_id=1, source_target_pairs={{0,32},{1,33},{2,34},{3,35},{4,36},{5,37},{6,38},{7,39},{8,40},{9,... | collective-permute-start | bytes 393224 | tf_op jit(solution)/shard_map/while/body/eval_jaxpr/ppermute | solution.py:13
  496.0 7.4 collective-permute-start.4
  534.1 10.9 %collective-permute-start.2 = (bf16[32,2048]{1,0:T(8,128)(2,1)S(1)}, bf16[32,2048]{1,0:T(8,128)(2,1)S(1)}, u32[]{:S(2)}, u32[]{:S(2)}) collective-permute-start(bf16[32,2048]{1,0:T(8,128)(2,1)S(1)} %maximum_select_fusion.18), channel_id=1, source_target_pairs={{0,32},{1,33},{2,34},{3,35},{4,36},{5,37},{6,38},{7,39},{8,40},{9,... | collective-permute-start | bytes 393224 | tf_op jit(solution)/shard_map/while/body/eval_jaxpr/ppermute | solution.py:13
  573.6 10.9 %collective-permute-start.3 = (bf16[32,2048]{1,0:T(8,128)(2,1)S(1)}, bf16[32,2048]{1,0:T(8,128)(2,1)S(1)}, u32[]{:S(2)}, u32[]{:S(2)}) collective-permute-start(bf16[32,2048]{1,0:T(8,128)(2,1)S(1)} %select_convert_fusion.6), channel_id=1, source_target_pairs={{0,32},{1,33},{2,34},{3,35},{4,36},{5,37},{6,38},{7,39},{8,40},{9,... | collective-permute-start | bytes 393224 | tf_op jit(solution)/shard_map/while/body/eval_jaxpr/ppermute | solution.py:13
  584.6 9.2 collective-permute-start.4
  621.2 11.2 %collective-permute-start.2 = (bf16[32,2048]{1,0:T(8,128)(2,1)S(1)}, bf16[32,2048]{1,0:T(8,128)(2,1)S(1)}, u32[]{:S(2)}, u32[]{:S(2)}) collective-permute-start(bf16[32,2048]{1,0:T(8,128)(2,1)S(1)} %maximum_select_fusion.18), channel_id=1, source_target_pairs={{0,32},{1,33},{2,34},{3,35},{4,36},{5,37},{6,38},{7,39},{8,40},{9,... | collective-permute-start | bytes 393224 | tf_op jit(solution)/shard_map/while/body/eval_jaxpr/ppermute | solution.py:13
  649.4 10.8 %collective-permute-start.3 = (bf16[32,2048]{1,0:T(8,128)(2,1)S(1)}, bf16[32,2048]{1,0:T(8,128)(2,1)S(1)}, u32[]{:S(2)}, u32[]{:S(2)}) collective-permute-start(bf16[32,2048]{1,0:T(8,128)(2,1)S(1)} %select_convert_fusion.6), channel_id=1, source_target_pairs={{0,32},{1,33},{2,34},{3,35},{4,36},{5,37},{6,38},{7,39},{8,40},{9,... | collective-permute-start | bytes 393224 | tf_op jit(solution)/shard_map/while/body/eval_jaxpr/ppermute | solution.py:13
  675.5 18.8 %collective-permute-start.6 = (bf16[8,2048]{1,0:T(8,128)(2,1)S(1)}, bf16[8,2048]{1,0:T(8,128)(2,1)}, u32[]{:S(2)}, u32[]{:S(2)}) collective-permute-start(bf16[8,2048]{1,0:T(8,128)(2,1)S(1)} %get-tuple-element.663), channel_id=1, source_target_pairs={{0,64},{64,128},{128,192},{1,65},{65,129},{129,193},{2,66},{66,130... | collective-permute-start | bytes 98312 | tf_op jit(solution)/shard_map/while/body/eval_jaxpr/ppermute | solution.py:19
  702.4 8.4 collective-permute-start.1
  710.8 12.7 %collective-permute-start.2 = (bf16[32,2048]{1,0:T(8,128)(2,1)S(1)}, bf16[32,2048]{1,0:T(8,128)(2,1)S(1)}, u32[]{:S(2)}, u32[]{:S(2)}) collective-permute-start(bf16[32,2048]{1,0:T(8,128)(2,1)S(1)} %maximum_select_fusion.18), channel_id=1, source_target_pairs={{0,32},{1,33},{2,34},{3,35},{4,36},{5,37},{6,38},{7,39},{8,40},{9,... | collective-permute-start | bytes 393224 | tf_op jit(solution)/shard_map/while/body/eval_jaxpr/ppermute | solution.py:13
  740.5 12.6 %collective-permute-start.3 = (bf16[32,2048]{1,0:T(8,128)(2,1)S(1)}, bf16[32,2048]{1,0:T(8,128)(2,1)S(1)}, u32[]{:S(2)}, u32[]{:S(2)}) collective-permute-start(bf16[32,2048]{1,0:T(8,128)(2,1)S(1)} %select_convert_fusion.6), channel_id=1, source_target_pairs={{0,32},{1,33},{2,34},{3,35},{4,36},{5,37},{6,38},{7,39},{8,40},{9,... | collective-permute-start | bytes 393224 | tf_op jit(solution)/shard_map/while/body/eval_jaxpr/ppermute | solution.py:13
  789.7 12.2 %collective-permute-start.2 = (bf16[32,2048]{1,0:T(8,128)(2,1)S(1)}, bf16[32,2048]{1,0:T(8,128)(2,1)S(1)}, u32[]{:S(2)}, u32[]{:S(2)}) collective-permute-start(bf16[32,2048]{1,0:T(8,128)(2,1)S(1)} %maximum_select_fusion.18), channel_id=1, source_target_pairs={{0,32},{1,33},{2,34},{3,35},{4,36},{5,37},{6,38},{7,39},{8,40},{9,... | collective-permute-start | bytes 393224 | tf_op jit(solution)/shard_map/while/body/eval_jaxpr/ppermute | solution.py:13
  818.8 12.1 %collective-permute-start.3 = (bf16[32,2048]{1,0:T(8,128)(2,1)S(1)}, bf16[32,2048]{1,0:T(8,128)(2,1)S(1)}, u32[]{:S(2)}, u32[]{:S(2)}) collective-permute-start(bf16[32,2048]{1,0:T(8,128)(2,1)S(1)} %select_convert_fusion.6), channel_id=1, source_target_pairs={{0,32},{1,33},{2,34},{3,35},{4,36},{5,37},{6,38},{7,39},{8,40},{9,... | collective-permute-start | bytes 393224 | tf_op jit(solution)/shard_map/while/body/eval_jaxpr/ppermute | solution.py:13
  846.3 13.9 %collective-permute-start.6 = (bf16[8,2048]{1,0:T(8,128)(2,1)S(1)}, bf16[8,2048]{1,0:T(8,128)(2,1)}, u32[]{:S(2)}, u32[]{:S(2)}) collective-permute-start(bf16[8,2048]{1,0:T(8,128)(2,1)S(1)} %get-tuple-element.663), channel_id=1, source_target_pairs={{0,64},{64,128},{128,192},{1,65},{65,129},{129,193},{2,66},{66,130... | collective-permute-start | bytes 98312 | tf_op jit(solution)/shard_map/while/body/eval_jaxpr/ppermute | solution.py:19
  (42 other events, 482.3 us)
Sparse Core Ops, SparseCore 0:
  865.3 94.6 all-reduce.1
where the time goes:
time: 976 us; the launch traced here: 968 us
  waiting for transfers between devices  406 us (42%)
  starting transfers between devices  304 us (31%)
  local copies, waits for them, and re-layouts  112 us (11%)
  other arithmetic  93.1 us (10%)
  matrix products  36.9 us (4%)
  between operations  14.2 us (1%)
    ppermute x52, waiting for transfers between devices, swapped(): lax.ppermute(value, axis, [(i, i ^ 1 << bit) for i in range(lax.axis_size...  310 us
    ppermute x52, starting transfers between devices, swapped(): lax.ppermute(value, axis, [(i, i ^ 1 << bit) for i in range(lax.axis_size...  255 us
    psum x1, waiting for transfers between devices, spread_2(): return lax.psum(jnp.where(mine, value, jnp.zeros_like(value)), axis)  94.8 us
    ppermute x7, starting transfers between devices, from_behind(): lax.ppermute(value, axis, [(source, source + steps) for source in range(i...  48.8 us
    mul x21, local copies, waits for them, and re-layouts, head_norm(): values * lax.rsqrt(jnp.mean(values * values, axis=-1, keepdims=True) + EP...  20 us
  transfers between devices with their start and end apart: 60, of which 53 were waited for; matrix products, arithmetic and copies ran while one was open for 3% of the time, Pallas kernels for 0%

commit v1 on v0

v1 whole, which is shorter than its diff:
```python
import functools
import math

import jax
import jax.numpy as jnp
from jax import lax
from jax.experimental import pallas as pl
from jax.experimental.pallas import tpu as pltpu
from jax.sharding import PartitionSpec as P

GUIDANCE_SCALE = 6.0
EPSILON = 1e-06
MESH = pl.DeviceIdType.MESH
F32 = jnp.float32
BF16 = jnp.bfloat16
NT = (((1,), (1,)), ((), ()))


def packed_rows(values):
    half = values.shape[-1] // 2
    return jnp.concatenate((values[..., :half], values[..., half:]), axis=-2)


def head_norm(values, gain_row):
    square = jnp.mean(values * values, axis=-1, keepdims=True)
    return values * lax.rsqrt(square + EPSILON) * gain_row


def kernel(
    sizes,
    latent,
    modulation,
    qkv_piece,
    out_piece,
    gains,
    stale,
    guided_out,
    own_kv,
    qkv_all,
    out_all,
    others,
    inputs,
    features,
    mixed_left,
    partials,
    arrived,
    finals,
    partner,
    guided_sent,
    z_send,
    z_recv,
    pair_send,
    pair_recv,
    gather_send,
    gather_recv,
    scatter_send,
    scatter_recv,
    pipe_send,
    pipe_recv,
    cfg_send,
    cfg_recv,
    guided_send,
    guided_recv,
):
    sections, slices, members, patches = sizes
    branch = lax.axis_index("cfg")
    section = lax.axis_index("pipe")
    rank = lax.axis_index("seq")
    y = rank // members
    z = rank % members
    rows = features.shape[1] * 8
    width = features.shape[3]
    middle = members // 2

    def at_y(index):
        return (branch, section, index * members + z)

    def at_z(index):
        return (branch, section, y * members + index)

    right = at_z((z + 1) % members)
    left = at_z((z + members - 1) % members)
    sibling = (1 - branch, section, rank)

    def at_pipe(index):
        return (branch, index, rank)

    barrier = pltpu.get_barrier_semaphore()
    greeted = [at_y((y + d) % slices) for d in range(1, slices)]
    greeted += [right, left, sibling]
    greeted += [at_pipe((section + d) % sections) for d in range(1, sections)]
    for device in greeted:
        pl.semaphore_signal(barrier, inc=1, device_id=device, device_id_type=MESH)
    pl.semaphore_wait(barrier, len(greeted))

    def remote(src, dst, send, recv, device):
        return pltpu.make_async_remote_copy(
            src_ref=src,
            dst_ref=dst,
            send_sem=send,
            recv_sem=recv,
            device_id=device,
            device_id_type=MESH,
        )

    def part(ref, step, way):
        if step < middle:
            return ref
        return ref.at[:, pl.ds(way * 1024, 1024)]

    def hop(step, way, item, lands=False):
        device = left if way else right
        sign = 1 if way else members - 1
        owner = (z + sign * (step - 1)) % members
        block = (z + sign * step) % members if lands else owner
        send, recv = z_send.at[item, way, step - 1], z_recv.at[item, way, step - 1]
        if item == 2:
            source = (step - 1 if way == 0 else members - step + 1) - 1
            target = (step if way == 0 else members - step) - 1
            here = stale if step == 1 else others.at[source]
            there = others.at[target]
            if step == middle:
                here, there = here.at[way], there.at[way]
        else:
            piece, full = (qkv_piece, qkv_all) if item == 0 else (out_piece, out_all)
            here = piece.at[branch] if step == 1 else full.at[owner * 2 + branch]
            here = part(here, step, way)
            there = part(full.at[block * 2 + branch], step, way)
        return remote(here, there, send, recv, device)

    def handed(step, way, item, lands=False):
        sign = 1 if way else members - 1
        landing = (z + sign * step) % members
        full = qkv_all if item == 0 else out_all
        send, recv = pair_send.at[item, way, step - 1], pair_recv.at[item, way, step - 1]
        half = 1 - branch if lands else branch
        block = part(full.at[landing * 2 + half], step, way)
        return remote(block, block, send, recv, sibling)

    for item in (0, 2, 1):
        for way in (0, 1):
            hop(1, way, item).start()

    for half in (0, 1):
        qkv_all[z * 2 + half] = qkv_piece[half]
        out_all[z * 2 + half] = out_piece[half]
    own_kv[...] = stale[...]

    @pl.when(section == 0)
    def _():
        inputs[...] = latent[...]

    for step in range(1, middle + 1):
        for item in (0, 2, 1):
            for way in (0, 1):
                hop(step, way, item, lands=True).wait_recv()
                if step < middle:
                    hop(step + 1, way, item).start()
                if item != 2:
                    handed(step, way, item).start()
    for step in range(1, middle + 1):
        for item in (0, 1):
            for way in (0, 1):
                handed(step, way, item, lands=True).wait_recv()

    order = [4, 3, 5, 2, 6, 1, 7] if slices == 8 else list(range(1, slices))

    def gather_copy(p, d):
        return remote(
            features.at[p, y],
            features.at[p, y],
            gather_send.at[p, d],
            gather_recv.at[p, d],
            at_y((y + d) % slices),
        )

    def gather_landing(p, d):
        return remote(
            features.at[p, y],
            features.at[p, (y + slices - d) % slices],
            gather_send.at[p, d],
            gather_recv.at[p, d],
            at_y((y + d) % slices),
        )

    def scatter_copy(p, d):
        return remote(
            partials.at[p, (y + d) % slices],
            arrived.at[p, d],
            scatter_send.at[p, d],
            scatter_recv.at[p, d],
            at_y((y + d) % slices),
        )

    def pipe_copy(p):
        return remote(
            finals.at[p],
            inputs.at[p],
            pipe_send.at[p],
            pipe_recv.at[p],
            at_pipe((section + 1) % sections),
        )

    def cfg_copy(p):
        return remote(finals.at[p], partner.at[p], cfg_send.at[p], cfg_recv.at[p], sibling)

    def both(left_rows):
        total = left_rows[:8] + left_rows[8:]
        return jnp.concatenate((total, total), axis=0)

    def start_patch(p):
        @pl.when(section > 0)
        def _():
            pipe_copy(p).wait_recv()

        x = inputs[p].astype(F32)
        count = 2 * width
        center = x - both(jnp.sum(x, axis=1, keepdims=True)) / count
        spread = both(jnp.sum(center * center, axis=1, keepdims=True)) / count
        normed = center * lax.rsqrt(spread + EPSILON)
        features[p, y] = (normed * (1.0 + modulation[1]) + modulation[0]).astype(BF16)
        for d in order:
            gather_copy(p, d).start()

    def attend(p):
        for d in order:
            gather_landing(p, d).wait_recv()
        stacked = features[p].astype(F32)
        mixed_left[0] = stacked[:, :8].reshape(rows, width).astype(BF16)
        mixed_left[1] = stacked[:, 8:].reshape(rows, width).astype(BF16)
        sums = []
        for head in range(2):
            total = None
            for piece in range(4):
                side, lane = piece // 2, (piece % 2) * 512
                weight = qkv_all[pl.ds(head * members, members), :, pl.ds(piece * 512, 512)]
                product = lax.dot_general(
                    mixed_left[side, :, pl.ds(lane, 512)],
                    weight.reshape(members * weight.shape[1], 512),
                    NT,
                    preferred_element_type=F32,
                )
                total = product if total is None else total + product
            sums.append(total)
        queries = [head_norm(m[:, :128], gains[0:1]).astype(BF16) for m in sums]
        keys = [head_norm(m[:, 128:256], gains[1:2]).astype(BF16) for m in sums]
        values = [m[:, 256:].astype(BF16) for m in sums]
        own_kv[0, p] = jnp.concatenate(keys, axis=1)
        own_kv[1, p] = jnp.concatenate(values, axis=1)
        attended = []
        scale = 1.0 / math.sqrt(128)
        for head in range(2):
            lanes = pl.ds(head * 128, 128)
            summed, weight_sum = None, None
            for member in range(members):
                block = own_kv if member == members - 1 else others.at[member]
                key_rows = block[0, :, :, lanes].reshape(patches * rows, 128)
                value_rows = block[1, :, :, lanes].reshape(patches * rows, 128)
                scores = lax.dot_general(
                    queries[head], key_rows, NT, preferred_element_type=F32
                )
                weights = jnp.exp(scores * scale)
                product = jnp.dot(
                    weights.astype(BF16), value_rows, preferred_element_type=F32
                )
                summed = product if summed is None else summed + product
                weight_sum = weights if weight_sum is None else weight_sum + weights
            attended.append(
                (summed / jnp.sum(weight_sum, axis=1, keepdims=True)).astype(BF16)
            )
        attended = jnp.concatenate(attended, axis=1)
        out_rows = members * 32
        for lane in range(0, width, 512):
            low = jnp.dot(
                attended,
                out_all[:, :, pl.ds(lane, 512)].reshape(out_rows, 512),
                preferred_element_type=F32,
            )
            high = jnp.dot(
                attended,
                out_all[:, :, pl.ds(width + lane, 512)].reshape(out_rows, 512),
                preferred_element_type=F32,
            )
            packed = jnp.concatenate(
                (low.reshape(slices, 8, 512), high.reshape(slices, 8, 512)), axis=1
            )
            partials[p, :, :, pl.ds(lane, 512)] = packed.astype(BF16)
        for d in order:
            scatter_copy(p, d).start()

    def finish_patch(p):
        total = partials[p, y].astype(F32)
        for d in reversed(order):
            scatter_copy(p, d).wait_recv()
            total = total + arrived[p, d].astype(F32)
        finals[p] = (inputs[p].astype(F32) + modulation[2] * total).astype(BF16)

        @pl.when(section < sections - 1)
        def _():
            pipe_copy(p).start()

        @pl.when(section == sections - 1)
        def _():
            cfg_copy(p).start()

    def guided_copy(p, device):
        return remote(
            guided_sent.at[p], guided_out, guided_send.at[p], guided_recv, at_pipe(device)
        )

    def guide(p):
        cfg_copy(p).wait_recv()
        own, other = finals[p].astype(F32), partner[p].astype(F32)
        first = branch == 0
        own = jnp.where(first, own[:8], own[8:])
        other = jnp.where(first, other[:8], other[8:])
        conditional = jnp.where(first, own, other)
        unconditional = jnp.where(first, other, own)
        guided = unconditional + GUIDANCE_SCALE * (conditional - unconditional)
        return packed_rows(guided).astype(BF16)

    start_patch(0)

    def tick(p, carry):
        attend(p)

        @pl.when(p < patches - 1)
        def _():
            start_patch(p + 1)

        finish_patch(p)

        @pl.when(jnp.logical_and(section == sections - 1, p > 0))
        def _():
            guided_sent[p - 1] = guide(p - 1)
            guided_copy(p - 1, p - 1).start()

        return carry

    lax.fori_loop(0, patches, tick, 0)

    @pl.when(section == sections - 1)
    def _():
        guided_out[...] = guide(patches - 1)

    @pl.when(section < sections - 1)
    def _():
        guided_copy(0, sections - 1).wait_recv()

    for step in range(1, middle + 1):
        for item in (0, 1, 2):
            for way in (0, 1):
                hop(step, way, item).wait_send()
                if item != 2:
                    handed(step, way, item).wait_send()

    def drain(p, carry):
        for d in order:
            gather_copy(p, d).wait_send()
            scatter_copy(p, d).wait_send()

        @pl.when(section < sections - 1)
        def _():
            pipe_copy(p).wait_send()

        @pl.when(section == sections - 1)
        def _():
            cfg_copy(p).wait_send()

        @pl.when(jnp.logical_and(section == sections - 1, p < patches - 1))
        def _():
            guided_copy(p, p).wait_send()

        return carry

    lax.fori_loop(0, patches, drain, 0)


def local(latent, modulation, qkv_weight, out_weight, norm_gain, stale_kv):
    patches, tok_dev, model_width = latent.shape
    sections = lax.axis_size("pipe")
    slices = 8
    members = lax.axis_size("seq") // slices
    half = model_width // 2
    group_rows = slices * tok_dev
    local_width = stale_kv.shape[7]
    packed = 2 * tok_dev
    latent_packed = (
        latent.reshape(patches, tok_dev, 2, half)
        .transpose(0, 2, 1, 3)
        .reshape(patches, packed, half)
    )
    modulation_packed = jnp.broadcast_to(
        modulation[0, 0].reshape(3, 2, 1, half), (3, 2, tok_dev, half)
    ).reshape(3, packed, half)
    qkv_piece = qkv_weight[0].T
    qkv_piece = qkv_piece.reshape(2, qkv_piece.shape[0] // 2, model_width)
    out_piece = out_weight[0]
    out_piece = out_piece.reshape(2, out_piece.shape[0] // 2, model_width)
    stale = stale_kv[0, 0].reshape(2, patches, group_rows, local_width)
    dma = pltpu.SemaphoreType.DMA
    vmem = pl.BlockSpec(memory_space=pltpu.VMEM)
    blocks = members * 2
    guided, own_kv = pl.pallas_call(
        functools.partial(kernel, (sections, slices, members, patches)),
        out_shape=(
            jax.ShapeDtypeStruct((packed, half // 2), BF16),
            jax.ShapeDtypeStruct(stale.shape, BF16),
        ),
        in_specs=[vmem] * 6,
        out_specs=(vmem, vmem),
        scratch_shapes=[
            pltpu.VMEM((blocks,) + qkv_piece.shape[1:], BF16),
            pltpu.VMEM((blocks,) + out_piece.shape[1:], BF16),
            pltpu.VMEM((members - 1,) + stale.shape, BF16),
            pltpu.VMEM((patches, packed, half), BF16),
            pltpu.VMEM((patches, slices, packed, half), BF16),
            pltpu.VMEM((2, group_rows, half), BF16),
            pltpu.VMEM((patches, slices, packed, half), BF16),
            pltpu.VMEM((patches, slices, packed, half), BF16),
            pltpu.VMEM((patches, packed, half), BF16),
            pltpu.VMEM((patches, packed, half), BF16),
            pltpu.VMEM((patches, packed, half // 2), BF16),
            dma((3, 2, 4)),
            dma((3, 2, 4)),
            dma((2, 2, 4)),
            dma((2, 2, 4)),
            dma((patches, slices)),
            dma((patches, slices)),
            dma((patches, slices)),
            dma((patches, slices)),
            dma((patches,)),
            dma((patches,)),
            dma((patches,)),
            dma((patches,)),
            dma((patches,)),
            dma(()),
        ],
        compiler_params=pltpu.CompilerParams(
            collective_id=0, has_side_effects=True, vmem_limit_bytes=50 * 2**20
        ),
    )(latent_packed, modulation_packed, qkv_piece, out_piece, norm_gain[0], stale)
    guided = (
        guided.reshape(2, tok_dev, half // 2)
        .transpose(1, 0, 2)
        .reshape(1, tok_dev, half)
    )
    return guided, own_kv.reshape(stale_kv.shape)


def solution(mesh):
    placed = (
        P(None, "seq", None),
        P("pipe", "cfg", None, None),
        P("pipe", None, "seq"),
        P("pipe", "seq", None),
        P("pipe", None, None),
        P("pipe", "cfg", None, None, "seq", None, None, None),
    )
    return jax.shard_map(
        local,
        mesh=mesh,
        in_specs=placed,
        out_specs=(P("pipe", "seq", "cfg"), P("pipe", "cfg", None, None, "seq", None, None, None)),
        check_vma=False,
    )
```

time: 976 us -> 198 us (0.20)
  the two profiles are of different devices: /device:TPU:32 before, /device:TPU:4 now
where the time goes in v1:
time: 198 us; the launch traced here: 197 us
  Pallas kernels  191 us (96%)
  local copies, waits for them, and re-layouts  4.83 us (2%)
    pallas_call x1, Pallas kernels, local(): pl.pallas_call(functools.partial(kernel, (sections, slices, members, patc...  191 us
    unnamed x12, local copies, waits for them, and re-layouts  4.78 us

profile of v1, /device:TPU:4, one launch (start us, length us, event | category | flops | bytes accessed | tf_op | source)
XLA Modules:
  0.0 197.4 jit_solution(143574604225391130)
XLA Ops:
  0.6 0.0 copy-start.1
  0.6 0.8 reduce
  1.5 0.0 copy-start.4
  1.6 0.0 copy-done.1
  1.6 0.6 copy-done.4
  2.2 0.0 copy-start
  2.2 1.0 copy-done
  3.2 0.0 copy-start.2
  3.2 0.9 copy-done.2
  4.1 0.0 copy-start.3
  4.1 0.9 copy-done.3
  5.0 191.0 %shard_map.77 = (bf16[16,512]{1,0:T(8,128)(2,1)S(1)}, bf16[2,4,64,256]{3,2,1,0:T(8,128)(2,1)S(1)}) custom-call(bf16[4,16,1024]{2,1,0:T(8,128)(2,1)S(1)} %bitcast.26, f32[3,16,1024]{2,1,0:T(8,128)S(1)} %broadcast_bitcast_fusion.modulation, bf16[2,48,2048]{2,1,0:T(8,128)(2,1)S(1)} %bitcast.23, bf16[2,16,2048]{2,1,0:T(8,128)(2,1)S(1)} %bitcast.27, ...), custom_call_target="tpu_custom_call" | custom-call | tf_op jit(solution)/shard_map/pallas_call | solution.py:404
  196.1 0.6 copy.11
  196.7 0.7 copy.12
  (2 shorter events, 0.0 us)
Async XLA Ops:
  0.6 1.0 copy-start.1
  1.5 0.7 copy-start.4
  2.2 1.0 copy-start
  3.2 0.9 copy-start.2
  4.1 0.9 copy-start.3

commit v2 on v1

v2 whole, which is shorter than its diff:
```python
import functools
import math

import jax
import jax.numpy as jnp
from jax import lax
from jax.experimental import pallas as pl
from jax.experimental.pallas import tpu as pltpu
from jax.sharding import PartitionSpec as P

GUIDANCE_SCALE = 6.0
EPSILON = 1e-06
MESH = pl.DeviceIdType.MESH
F32 = jnp.float32
BF16 = jnp.bfloat16
NT = (((1,), (1,)), ((), ()))


def packed_rows(values):
    half = values.shape[-1] // 2
    return jnp.concatenate((values[..., :half], values[..., half:]), axis=-2)


def head_norm(values, gain_row):
    square = jnp.mean(values * values, axis=-1, keepdims=True)
    return values * lax.rsqrt(square + EPSILON) * gain_row


def kernel(
    sizes,
    latent,
    modulation,
    qkv_piece,
    out_piece,
    norm_gain,
    stale,
    guided_out,
    own_kv,
    qkv_all,
    out_all,
    caches,
    raw_modulation,
    gains,
    shift,
    scale,
    gate,
    inputs,
    residuals,
    features,
    mixed_left,
    queries,
    fresh,
    partials,
    arrived,
    finals,
    partner,
    guided_sent,
    local_sem,
    z_send,
    z_recv,
    pair_send,
    pair_recv,
    gather_send,
    gather_recv,
    scatter_send,
    scatter_recv,
    pipe_send,
    pipe_recv,
    cfg_send,
    cfg_recv,
    guided_send,
    guided_recv,
):
    sections, slices, members, patches = sizes
    branch = lax.axis_index("cfg")
    section = lax.axis_index("pipe")
    rank = lax.axis_index("seq")
    y = rank // members
    z = rank % members
    rows = features.shape[1] * 8
    width = features.shape[3]
    middle = members // 2
    is_first = section == 0
    is_last = section == sections - 1

    local_copies = [
        pltpu.make_async_copy(src, dst, local_sem.at[n])
        for n, (src, dst) in enumerate(
            (
                (qkv_piece, qkv_all.at[pl.ds(z * 2, 2)]),
                (stale, caches.at[0]),
                (out_piece, out_all.at[pl.ds(z * 2, 2)]),
                (modulation, raw_modulation),
                (norm_gain, gains),
                (stale, own_kv),
                (latent, inputs),
            )
        )
    ]
    for copy in local_copies[:-1]:
        copy.start()
    pl.when(is_first)(local_copies[-1].start)

    def at_z(index):
        return (branch, section, y * members + index)

    right = at_z((z + 1) % members)
    left = at_z((z + members - 1) % members)
    sibling = (1 - branch, section, rank)

    def at(plane, d):
        return (branch, plane, (y + d) % slices * members + z)

    following = (section + 1) % sections
    barrier = pltpu.get_barrier_semaphore()
    greeted = [right, left, sibling] + [at(section, d) for d in range(1, slices)]
    for d in range(slices):
        greeted += [at(following, d), at((section + sections - 1) % sections, d)]
    greeted += [at((section + d) % sections, 0) for d in range(2, sections - 1)]
    for device in greeted:
        pl.semaphore_signal(barrier, inc=1, device_id=device, device_id_type=MESH)
    pl.semaphore_wait(barrier, len(greeted))

    def remote(src, dst, send, recv, device):
        return pltpu.make_async_remote_copy(
            src_ref=src,
            dst_ref=dst,
            send_sem=send,
            recv_sem=recv,
            device_id=device,
            device_id_type=MESH,
        )

    def block(item, step, way, half, distance):
        if item in (2, 3):
            slot = distance if way == 0 else (members - distance) % members
            return caches.at[slot, item - 2]
        sign = 1 if way else members - 1
        owner = (z + sign * distance) % members
        if item == 4:
            ref = out_all.at[owner * 2 + half]
            return ref if step < middle else ref.at[:, pl.ds(way * 1024, 1024)]
        return qkv_all.at[owner * 2 + half, :, pl.ds(item * 1024, 1024)]

    def ways(item, step):
        return (0, 1) if step < middle or item == 4 else (item % 2,)

    def hop(item, step, way, lands=False):
        here = block(item, step, way, branch, step - 1)
        if item in (2, 3) or lands:
            there = block(item, step, way, branch, step)
        else:
            there = here
        send, recv = z_send.at[item, way, step - 1], z_recv.at[item, way, step - 1]
        return remote(here, there, send, recv, left if way else right)

    def handed(item, step, way, lands=False):
        ref = block(item, step, way, 1 - branch if lands else branch, step)
        send, recv = pair_send.at[item, way, step - 1], pair_recv.at[item, way, step - 1]
        return remote(ref, ref, send, recv, sibling)

    def land(item, step):
        for way in ways(item, step):
            hop(item, step, way, lands=True).wait_recv()
            if step < middle and way in ways(item, step + 1):
                hop(item, step + 1, way).start()
            if item not in (2, 3):
                handed(item, step, way).start()

    def take_handed(item):
        for step in range(1, middle + 1):
            for way in ways(item, step):
                handed(item, step, way, lands=True).wait_recv()

    items = (0, 1, 2, 3, 4)
    loaded = set()
    for item in items:
        copy = (0, 0, 1, 1, 2)[item]
        if copy not in loaded:
            local_copies[copy].wait()
            loaded.add(copy)
        for way in ways(item, 1):
            hop(item, 1, way).start()

    order = [4, 3, 5, 2, 6, 1, 7] if slices == 8 else list(range(1, slices))

    def gather_copy(p, d):
        return remote(
            features.at[p, y],
            features.at[p, y],
            gather_send.at[p, d],
            gather_recv.at[p, d],
            at(section, d),
        )

    def gather_landing(p, d):
        return remote(
            features.at[p, y],
            features.at[p, (y + slices - d) % slices],
            gather_send.at[p, d],
            gather_recv.at[p, d],
            at(section, d),
        )

    def scatter_copy(p, d, last):
        return remote(
            partials.at[p, (y + d) % slices],
            arrived.at[last, p, d],
            scatter_send.at[p, d],
            scatter_recv.at[last, p, d],
            at(section if last else following, d),
        )

    def pipe_copy(p):
        return remote(
            inputs.at[p], residuals.at[p], pipe_send.at[p], pipe_recv.at[p], at(following, 0)
        )

    def cfg_copy(p):
        return remote(finals.at[p], partner.at[p], cfg_send.at[p], cfg_recv.at[p], sibling)

    def both(left_rows):
        total = left_rows[:8] + left_rows[8:]
        return jnp.concatenate((total, total), axis=0)

    def start_patch(p):
        @pl.when(jnp.logical_not(is_first))
        def _():
            pipe_copy(p).wait_recv()
            total = residuals[p].astype(F32)
            for d in [0] + order[::-1]:
                scatter_copy(p, d, 0).wait_recv()
                total = total + arrived[0, p, d].astype(F32)
            inputs[p] = total.astype(BF16)

        x = inputs[p].astype(F32)
        count = 2 * width
        center = x - both(jnp.sum(x, axis=1, keepdims=True)) / count
        spread = both(jnp.sum(center * center, axis=1, keepdims=True)) / count
        normed = center * lax.rsqrt(spread + EPSILON)
        features[p, y] = (normed * scale[...] + shift[...]).astype(BF16)
        for d in order:
            gather_copy(p, d).start()
        pl.when(jnp.logical_not(is_last))(lambda: pipe_copy(p).start())

    def project(p):
        for d in order:
            gather_landing(p, d).wait_recv()
        stacked = features[p].astype(F32)
        mixed_left[0] = stacked[:, :8].reshape(rows, width).astype(BF16)
        mixed_left[1] = stacked[:, 8:].reshape(rows, width).astype(BF16)
        for head in range(2):
            total = None
            for piece in range(4):
                side, lane = piece // 2, (piece % 2) * 512
                weight = qkv_all[pl.ds(head * members, members), :, pl.ds(piece * 512, 512)]
                product = lax.dot_general(
                    mixed_left[side, :, pl.ds(lane, 512)],
                    weight.reshape(members * weight.shape[1], 512),
                    NT,
                    preferred_element_type=F32,
                )
                total = product if total is None else total + product
            lanes = pl.ds(head * 128, 128)
            queries[p, :, lanes] = head_norm(total[:, :128], gains[0:1]).astype(BF16)
            fresh[p, 0, :, lanes] = head_norm(total[:, 128:256], gains[1:2]).astype(BF16)
            fresh[p, 1, :, lanes] = total[:, 256:].astype(BF16)

    def attend(p):
        own_kv[0, p] = fresh[p, 0]
        own_kv[1, p] = fresh[p, 1]
        attended = []
        factor = 1.0 / math.sqrt(128)
        for head in range(2):
            lanes = pl.ds(head * 128, 128)
            query = queries[p, :, lanes]
            summed, weight_sum = None, None
            for member in range(members):
                rows_of = own_kv if member == 0 else caches.at[member]
                key_rows = rows_of[0, :, :, lanes].reshape(patches * rows, 128)
                value_rows = rows_of[1, :, :, lanes].reshape(patches * rows, 128)
                scores = lax.dot_general(query, key_rows, NT, preferred_element_type=F32)
                weights = jnp.exp(scores * factor)
                product = jnp.dot(
                    weights.astype(BF16), value_rows, preferred_element_type=F32
                )
                summed = product if summed is None else summed + product
                weight_sum = weights if weight_sum is None else weight_sum + weights
            attended.append(
                (summed / jnp.sum(weight_sum, axis=1, keepdims=True)).astype(BF16)
            )
        attended = jnp.concatenate(attended, axis=1)
        out_rows = members * 32
        for lane in range(0, width, 512):
            sides = []
            for start in (lane, width + lane):
                product = jnp.dot(
                    attended,
                    out_all[:, :, pl.ds(start, 512)].reshape(out_rows, 512),
                    preferred_element_type=F32,
                )
                sides.append(product.reshape(slices, 8, 512) * gate[:, pl.ds(start, 512)])
            packed = jnp.concatenate(sides, axis=1)
            partials[p, :, :, pl.ds(lane, 512)] = packed.astype(BF16)

        @pl.when(is_last)
        def _():
            for d in order:
                scatter_copy(p, d, 1).start()

        @pl.when(jnp.logical_not(is_last))
        def _():
            for d in order + [0]:
                scatter_copy(p, d, 0).start()

    def finish_patch(p):
        total = inputs[p].astype(F32) + partials[p, y].astype(F32)
        for d in reversed(order):
            scatter_copy(p, d, 1).wait_recv()
            total = total + arrived[1, p, d].astype(F32)
        finals[p] = total.astype(BF16)
        cfg_copy(p).start()

    def guided_copy(p, device):
        return remote(
            guided_sent.at[p], guided_out, guided_send.at[p], guided_recv, at(device, 0)
        )

    def guide(p):
        cfg_copy(p).wait_recv()
        own, other = finals[p].astype(F32), partner[p].astype(F32)
        first = branch == 0
        own = jnp.where(first, own[:8], own[8:])
        other = jnp.where(first, other[:8], other[8:])
        conditional = jnp.where(first, own, other)
        unconditional = jnp.where(first, other, own)
        guided = unconditional + GUIDANCE_SCALE * (conditional - unconditional)
        return packed_rows(guided).astype(BF16)

    def send_guided(p):
        guided_sent[p] = guide(p)
        guided_copy(p, p).start()

    local_copies[3].wait()
    for lane in range(16):
        lanes = pl.ds(lane % 8 * 128, 128)
        half = pl.ds(lane // 8 * 8, 8)
        row = lambda kind: jnp.broadcast_to(raw_modulation[pl.ds(kind * 16 + lane, 1), :], (8, 128))
        shift[half, lanes] = row(0)
        scale[half, lanes] = 1.0 + row(1)
        gate[:, pl.ds(lane * 128, 128)] = row(2)

    def each_patch(body):
        def step(p, carry):
            body(p)
            return carry

        lax.fori_loop(0, patches, step, 0)

    @pl.when(is_first)
    def _():
        local_copies[-1].wait()
        each_patch(start_patch)

    for step in range(1, middle + 1):
        for item in items:
            if step == middle and item in (2, 3):
                continue
            land(item, step)
    take_handed(0)
    take_handed(1)
    local_copies[4].wait()
    pl.when(is_first)(lambda: each_patch(project))
    for item in (2, 3):
        land(item, middle)
    take_handed(4)
    local_copies[5].wait()

    def tick(p):
        @pl.when(jnp.logical_not(is_first))
        def _():
            pl.when(p < patches - 1)(lambda: start_patch(p + 1))
            project(p)

        attend(p)

        @pl.when(jnp.logical_and(is_last, p > 0))
        def _():
            finish_patch(p - 1)

        @pl.when(jnp.logical_and(is_last, p > 1))
        def _():
            send_guided(p - 2)

    pl.when(jnp.logical_not(is_first))(lambda: start_patch(0))
    each_patch(tick)

    @pl.when(is_last)
    def _():
        finish_patch(patches - 1)
        send_guided(patches - 2)
        guided_out[...] = guide(patches - 1)

    @pl.when(jnp.logical_not(is_last))
    def _():
        guided_copy(0, sections - 1).wait_recv()

    for step in range(1, middle + 1):
        for item in items:
            for way in ways(item, step):
                hop(item, step, way).wait_send()
                if item not in (2, 3):
                    handed(item, step, way).wait_send()

    def drain(p):
        for d in order:
            gather_copy(p, d).wait_send()

        @pl.when(jnp.logical_not(is_last))
        def _():
            pipe_copy(p).wait_send()
            for d in order + [0]:
                scatter_copy(p, d, 0).wait_send()

        @pl.when(is_last)
        def _():
            cfg_copy(p).wait_send()
            for d in order:
                scatter_copy(p, d, 1).wait_send()

        @pl.when(jnp.logical_and(is_last, p < patches - 1))
        def _():
            guided_copy(p, p).wait_send()

    each_patch(drain)


def local(latent, modulation, qkv_weight, out_weight, norm_gain, stale_kv):
    patches, tok_dev, model_width = latent.shape
    sections = lax.axis_size("pipe")
    slices = 8
    members = lax.axis_size("seq") // slices
    half = model_width // 2
    group_rows = slices * tok_dev
    local_width = stale_kv.shape[7]
    packed = 2 * tok_dev
    latent_packed = (
        latent.reshape(patches, tok_dev, 2, half)
        .transpose(0, 2, 1, 3)
        .reshape(patches, packed, half)
    )
    modulation_rows = modulation.reshape(3 * model_width // 128, 128)
    qkv_piece = qkv_weight[0].T
    qkv_piece = qkv_piece.reshape(2, qkv_piece.shape[0] // 2, model_width)
    out_piece = out_weight[0]
    out_piece = out_piece.reshape(2, out_piece.shape[0] // 2, model_width)
    stale = stale_kv[0, 0].reshape(2, patches, group_rows, local_width)
    dma = pltpu.SemaphoreType.DMA
    vmem = pl.BlockSpec(memory_space=pltpu.VMEM)
    blocks = members * 2
    guided, own_kv = pl.pallas_call(
        functools.partial(kernel, (sections, slices, members, patches)),
        out_shape=(
            jax.ShapeDtypeStruct((packed, half // 2), BF16),
            jax.ShapeDtypeStruct(stale.shape, BF16),
        ),
        in_specs=[pl.BlockSpec(memory_space=pltpu.HBM)] * 6,
        out_specs=(vmem, vmem),
        scratch_shapes=[
            pltpu.VMEM((blocks,) + qkv_piece.shape[1:], BF16),
            pltpu.VMEM((blocks,) + out_piece.shape[1:], BF16),
            pltpu.VMEM((members,) + stale.shape, BF16),
            pltpu.VMEM(modulation_rows.shape, F32),
            pltpu.VMEM(norm_gain.shape[1:], F32),
            pltpu.VMEM((packed, half), F32),
            pltpu.VMEM((packed, half), F32),
            pltpu.VMEM((tok_dev, model_width), F32),
            pltpu.VMEM((patches, packed, half), BF16),
            pltpu.VMEM((patches, packed, half), BF16),
            pltpu.VMEM((patches, slices, packed, half), BF16),
            pltpu.VMEM((2, group_rows, half), BF16),
            pltpu.VMEM((patches, group_rows, local_width), BF16),
            pltpu.VMEM((patches, 2, group_rows, local_width), BF16),
            pltpu.VMEM((patches, slices, packed, half), BF16),
            pltpu.VMEM((2, patches, slices, packed, half), BF16),
            pltpu.VMEM((patches, packed, half), BF16),
            pltpu.VMEM((patches, packed, half), BF16),
            pltpu.VMEM((patches, packed, half // 2), BF16),
            dma((7,)),
            dma((5, 2, 4)),
            dma((5, 2, 4)),
            dma((5, 2, 4)),
            dma((5, 2, 4)),
            dma((patches, slices)),
            dma((patches, slices)),
            dma((patches, slices)),
            dma((2, patches, slices)),
            dma((patches,)),
            dma((patches,)),
            dma((patches,)),
            dma((patches,)),
            dma((patches,)),
            dma(()),
        ],
        compiler_params=pltpu.CompilerParams(
            collective_id=0, has_side_effects=True, vmem_limit_bytes=63 * 2**20 + 2**19
        ),
    )(latent_packed, modulation_rows, qkv_piece, out_piece, norm_gain[0], stale)
    guided = (
        guided.reshape(2, tok_dev, half // 2)
        .transpose(1, 0, 2)
        .reshape(1, tok_dev, half)
    )
    return guided, own_kv.reshape(stale_kv.shape)


def solution(mesh):
    placed = (
        P(None, "seq", None),
        P("pipe", "cfg", None, None),
        P("pipe", None, "seq"),
        P("pipe", "seq", None),
        P("pipe", None, None),
        P("pipe", "cfg", None, None, "seq", None, None, None),
    )
    return jax.shard_map(
        local,
        mesh=mesh,
        in_specs=placed,
        out_specs=(P("pipe", "seq", "cfg"), P("pipe", "cfg", None, None, "seq", None, None, None)),
        check_vma=False,
    )
```

time: 198 us -> 183 us (0.924)
  Pallas kernels: 191 us -> 179 us
    pallas_call x1, Pallas kernels: 191 us -> 179 us  [local(): pl.pallas_call(functools.partial(kernel, (sections, slices, members, patc...]
    unnamed x12 -> x2, local copies, waits for them, and re-layouts: 4.78 us -> 2.99 us
where the time goes in v2:
time: 183 us
  Pallas kernels  179 us (98%)
  local copies, waits for them, and re-layouts  2.99 us (2%)
    pallas_call x1, Pallas kernels, local(): pl.pallas_call(functools.partial(kernel, (sections, slices, members, patc...  179 us

profile of v2, /device:TPU:4, one launch (start us, length us, event | category | flops | bytes accessed | tf_op | source)
XLA Modules:
  0.0 182.8 jit_solution(2743779181680557492)
XLA Ops:
  0.6 179.1 %shard_map.77 = (bf16[16,512]{1,0:T(8,128)(2,1)}, bf16[2,4,64,256]{3,2,1,0:T(8,128)(2,1)}) custom-call(bf16[4,16,1024]{2,1,0:T(8,128)(2,1)} %bitcast.25, f32[48,128]{1,0:T(8,128)} %bitcast.27, bf16[2,48,2048]{2,1,0:T(8,128)(2,1)} %bitcast.22, bf16[2,16,2048]{2,1,0:T(8,128)(2,1)} %bitcast.26, f32[2,128]{1,0:T(2,128)} %bitcast.29, bf16[2,4,64,256]{3,2,1,0:T(8,128)(2,1)} %bitcast.23), custom_call_target="tpu_custom_call" | custom-call | tf_op jit(solution)/shard_map/pallas_call | solution.py:461
  179.8 1.3 copy.11
  181.1 1.7 copy.12

commit v3 on v2

--- a/solution.py
+++ b/solution.py
@@ -39,6 +39,7 @@
     qkv_all,
     out_all,
     caches,
+    helped,
     raw_modulation,
     gains,
     shift,
@@ -60,6 +61,8 @@
     z_recv,
     pair_send,
     pair_recv,
+    help_send,
+    help_recv,
     gather_send,
     gather_recv,
     scatter_send,
@@ -132,9 +135,9 @@
         )
 
     def block(item, step, way, half, distance):
-        if item in (2, 3):
+        if item in (2, 3, 5):
             slot = distance if way == 0 else (members - distance) % members
-            return caches.at[slot, item - 2]
+            return helped.at[slot] if item == 5 else caches.at[slot, item - 2]
         sign = 1 if way else members - 1
         owner = (z + sign * distance) % members
         if item == 4:
@@ -147,7 +150,7 @@
 
     def hop(item, step, way, lands=False):
         here = block(item, step, way, branch, step - 1)
-        if item in (2, 3) or lands:
+        if item in (2, 3, 5) or lands:
             there = block(item, step, way, branch, step)
         else:
             there = here
@@ -159,12 +162,24 @@
         send, recv = pair_send.at[item, way, step - 1], pair_recv.at[item, way, step - 1]
         return remote(ref, ref, send, recv, sibling)
 
+    def help_out():
+        return remote(
+            caches.at[0, 1], helped.at[0], help_send.at[0], help_recv.at[0], at(sections - 1, 0)
+        )
+
+    def help_back(slot):
+        return remote(
+            helped.at[slot], caches.at[slot, 1], help_send.at[slot], help_recv.at[slot], at(0, 0)
+        )
+
     def land(item, step):
         for way in ways(item, step):
             hop(item, step, way, lands=True).wait_recv()
             if step < middle and way in ways(item, step + 1):
                 hop(item, step + 1, way).start()
-            if item not in (2, 3):
+            if item == 5:
+                help_back(step if way == 0 else members - step).start()
+            elif item not in (2, 3):
                 handed(item, step, way).start()
 
     def take_handed(item):
@@ -173,14 +188,26 @@
                 handed(item, step, way, lands=True).wait_recv()
 
     items = (0, 1, 2, 3, 4)
-    loaded = set()
+    def here(item):
+        return jnp.logical_not(is_first) if item == 3 else section >= 0
+
+    for n in range(3):
+        local_copies[n].wait()
+    pl.when(is_first)(lambda: help_out().start())
+
+    @pl.when(is_last)
+    def _():
+        help_out().wait_recv()
+        for way in ways(5, 1):
+            hop(5, 1, way).start()
+        for step in range(1, middle + 1):
+            land(5, step)
+
     for item in items:
-        copy = (0, 0, 1, 1, 2)[item]
-        if copy not in loaded:
-            local_copies[copy].wait()
-            loaded.add(copy)
-        for way in ways(item, 1):
-            hop(item, 1, way).start()
+        @pl.when(here(item))
+        def _():
+            for way in ways(item, 1):
+                hop(item, 1, way).start()
 
     order = [4, 3, 5, 2, 6, 1, 7] if slices == 8 else list(range(1, slices))
 
@@ -366,21 +393,27 @@
         for item in items:
             if step == middle and item in (2, 3):
                 continue
-            land(item, step)
+            pl.when(here(item))(functools.partial(land, item, step))
     take_handed(0)
     take_handed(1)
     local_copies[4].wait()
     pl.when(is_first)(lambda: each_patch(project))
-    for item in (2, 3):
-        land(item, middle)
+    land(2, middle)
+    pl.when(here(3))(functools.partial(land, 3, middle))
+
+    @pl.when(is_first)
+    def _():
+        for slot in range(1, members):
+            help_back(slot).wait_recv()
+
     take_handed(4)
     local_copies[5].wait()
 
     def tick(p):
         @pl.when(jnp.logical_not(is_first))
         def _():
+            project(p)
             pl.when(p < patches - 1)(lambda: start_patch(p + 1))
-            project(p)
 
         attend(p)
 
@@ -405,12 +438,22 @@
     def _():
         guided_copy(0, sections - 1).wait_recv()
 
-    for step in range(1, middle + 1):
-        for item in items:
+    def drain_ring(item):
+        for step in range(1, middle + 1):
             for way in ways(item, step):
                 hop(item, step, way).wait_send()
-                if item not in (2, 3):
+                if item not in (2, 3, 5):
                     handed(item, step, way).wait_send()
+
+    for item in items:
+        pl.when(here(item))(functools.partial(drain_ring, item))
+    pl.when(is_first)(lambda: help_out().wait_send())
+
+    @pl.when(is_last)
+    def _():
+        drain_ring(5)
+        for slot in range(1, members):
+            help_back(slot).wait_send()
 
     def drain(p):
         for d in order:
@@ -470,6 +513,7 @@
             pltpu.VMEM((blocks,) + qkv_piece.shape[1:], BF16),
             pltpu.VMEM((blocks,) + out_piece.shape[1:], BF16),
             pltpu.VMEM((members,) + stale.shape, BF16),
+            pltpu.VMEM((members,) + stale.shape[1:], BF16),
             pltpu.VMEM(modulation_rows.shape, F32),
             pltpu.VMEM(norm_gain.shape[1:], F32),
             pltpu.VMEM((packed, half), F32),
@@ -487,10 +531,12 @@
             pltpu.VMEM((patches, packed, half), BF16),
             pltpu.VMEM((patches, packed, half // 2), BF16),
             dma((7,)),
-            dma((5, 2, 4)),
-            dma((5, 2, 4)),
-            dma((5, 2, 4)),
-            dma((5, 2, 4)),
+            dma((6, 2, 4)),
+            dma((6, 2, 4)),
+            dma((6, 2, 4)),
+            dma((6, 2, 4)),
+            dma((members,)),
+            dma((members,)),
             dma((patches, slices)),
             dma((patches, slices)),
             dma((patches, slices)),

time: 183 us -> 176 us (0.962)
  the two profiles are of different devices: /device:TPU:4 before, /device:TPU:12 now
where the time goes in v3:
time: 176 us
  Pallas kernels  172 us (98%)
  local copies, waits for them, and re-layouts  2.99 us (2%)
    pallas_call x1, Pallas kernels, local(): pl.pallas_call(functools.partial(kernel, (sections, slices, members, patc...  172 us

profile of v3, /device:TPU:12, one launch (start us, length us, event | category | flops | bytes accessed | tf_op | source)
XLA Modules:
  0.0 176.0 jit_solution(10562017082728027871)
XLA Ops:
  0.6 172.4 %shard_map.77 = (bf16[16,512]{1,0:T(8,128)(2,1)}, bf16[2,4,64,256]{3,2,1,0:T(8,128)(2,1)}) custom-call(bf16[4,16,1024]{2,1,0:T(8,128)(2,1)} %bitcast.25, f32[48,128]{1,0:T(8,128)} %bitcast.27, bf16[2,48,2048]{2,1,0:T(8,128)(2,1)} %bitcast.22, bf16[2,16,2048]{2,1,0:T(8,128)(2,1)} %bitcast.26, f32[2,128]{1,0:T(2,128)} %bitcast.29, bf16[2,4,64,256]{3,2,1,0:T(8,128)(2,1)} %bitcast.23), custom_call_target="tpu_custom_call" | custom-call | tf_op jit(solution)/shard_map/pallas_call | solution.py:504
  173.0 1.3 copy.11
  174.3 1.7 copy.12

commit v4 on v3

--- a/solution.py
+++ b/solution.py
@@ -289,33 +289,41 @@
                 )
                 total = product if total is None else total + product
             lanes = pl.ds(head * 128, 128)
-            queries[p, :, lanes] = head_norm(total[:, :128], gains[0:1]).astype(BF16)
+            queries[p, pl.ds(head * rows, rows), lanes] = head_norm(total[:, :128], gains[0:1]).astype(BF16)
             fresh[p, 0, :, lanes] = head_norm(total[:, 128:256], gains[1:2]).astype(BF16)
             fresh[p, 1, :, lanes] = total[:, 256:].astype(BF16)
 
     def attend(p):
         own_kv[0, p] = fresh[p, 0]
         own_kv[1, p] = fresh[p, 1]
-        attended = []
-        factor = 1.0 / math.sqrt(128)
-        for head in range(2):
-            lanes = pl.ds(head * 128, 128)
-            query = queries[p, :, lanes]
-            summed, weight_sum = None, None
-            for member in range(members):
-                rows_of = own_kv if member == 0 else caches.at[member]
-                key_rows = rows_of[0, :, :, lanes].reshape(patches * rows, 128)
-                value_rows = rows_of[1, :, :, lanes].reshape(patches * rows, 128)
-                scores = lax.dot_general(query, key_rows, NT, preferred_element_type=F32)
-                weights = jnp.exp(scores * factor)
+        factor = math.log2(math.e) / math.sqrt(128)
+        query = queries[p]
+        summed, weight_sum = None, None
+        for first in range(0, members, 4):
+            blocks = [own_kv if n == 0 else caches.at[n] for n in range(first, first + 4)]
+            scores = [
+                lax.dot_general(
+                    query,
+                    block[0].reshape(patches * rows, 256),
+                    NT,
+                    preferred_element_type=F32,
+                )
+                for block in blocks
+            ]
+            for block, score in zip(blocks, scores):
+                weights = jnp.exp2(score * factor)
                 product = jnp.dot(
-                    weights.astype(BF16), value_rows, preferred_element_type=F32
+                    weights.astype(BF16),
+                    block[1].reshape(patches * rows, 256),
+                    preferred_element_type=F32,
                 )
                 summed = product if summed is None else summed + product
                 weight_sum = weights if weight_sum is None else weight_sum + weights
-            attended.append(
-                (summed / jnp.sum(weight_sum, axis=1, keepdims=True)).astype(BF16)
-            )
+        weight_sum = jnp.sum(weight_sum, axis=1, keepdims=True)
+        attended = [
+            (summed[:rows, :128] / weight_sum[:rows]).astype(BF16),
+            (summed[rows:, 128:] / weight_sum[rows:]).astype(BF16),
+        ]
         attended = jnp.concatenate(attended, axis=1)
         out_rows = members * 32
         for lane in range(0, width, 512):
@@ -376,6 +384,8 @@
         shift[half, lanes] = row(0)
         scale[half, lanes] = 1.0 + row(1)
         gate[:, pl.ds(lane * 128, 128)] = row(2)
+
+    queries[...] = jnp.zeros_like(queries)
 
     def each_patch(body):
         def step(p, carry):
@@ -523,7 +533,7 @@
             pltpu.VMEM((patches, packed, half), BF16),
             pltpu.VMEM((patches, slices, packed, half), BF16),
             pltpu.VMEM((2, group_rows, half), BF16),
-            pltpu.VMEM((patches, group_rows, local_width), BF16),
+            pltpu.VMEM((patches, 2 * group_rows, local_width), BF16),
             pltpu.VMEM((patches, 2, group_rows, local_width), BF16),
             pltpu.VMEM((patches, slices, packed, half), BF16),
             pltpu.VMEM((2, patches, slices, packed, half), BF16),

time: 176 us -> 174 us (0.989)
  the two profiles are of different devices: /device:TPU:12 before, /device:TPU:4 now
where the time goes in v4:
time: 174 us; the launch traced here: 173 us
  Pallas kernels  170 us (98%)
  local copies, waits for them, and re-layouts  2.99 us (2%)
    pallas_call x1, Pallas kernels, local(): pl.pallas_call(functools.partial(kernel, (sections, slices, members, patc...  170 us

profile of v4, /device:TPU:4, one launch (start us, length us, event | category | flops | bytes accessed | tf_op | source)
XLA Modules:
  0.0 173.3 jit_solution(8624412926959853849)
XLA Ops:
  0.6 169.7 %shard_map.77 = (bf16[16,512]{1,0:T(8,128)(2,1)}, bf16[2,4,64,256]{3,2,1,0:T(8,128)(2,1)}) custom-call(bf16[4,16,1024]{2,1,0:T(8,128)(2,1)} %bitcast.25, f32[48,128]{1,0:T(8,128)} %bitcast.27, bf16[2,48,2048]{2,1,0:T(8,128)(2,1)} %bitcast.22, bf16[2,16,2048]{2,1,0:T(8,128)(2,1)} %bitcast.26, f32[2,128]{1,0:T(2,128)} %bitcast.29, bf16[2,4,64,256]{3,2,1,0:T(8,128)(2,1)} %bitcast.23), custom_call_target="tpu_custom_call" | custom-call | tf_op jit(solution)/shard_map/pallas_call | solution.py:514
  170.3 1.3 copy.11
  171.7 1.7 copy.12

commit v5 on v4

--- a/solution.py
+++ b/solution.py
@@ -200,7 +200,7 @@
         help_out().wait_recv()
         for way in ways(5, 1):
             hop(5, 1, way).start()
-        for step in range(1, middle + 1):
+        for step in range(1, 3 + 1):
             land(5, step)
 
     for item in items:
@@ -208,6 +208,11 @@
         def _():
             for way in ways(item, 1):
                 hop(item, 1, way).start()
+
+    @pl.when(is_last)
+    def _():
+        for step in range(3 + 1, middle + 1):
+            land(5, step)
 
     order = [4, 3, 5, 2, 6, 1, 7] if slices == 8 else list(range(1, slices))
 
@@ -274,15 +279,17 @@
         for d in order:
             gather_landing(p, d).wait_recv()
         stacked = features[p].astype(F32)
-        mixed_left[0] = stacked[:, :8].reshape(rows, width).astype(BF16)
-        mixed_left[1] = stacked[:, 8:].reshape(rows, width).astype(BF16)
+        halves = [
+            stacked[:, 8 * side : 8 * side + 8] for side in (0, 1)
+        ]
+        halves = [half.reshape(rows, width).astype(BF16) for half in halves]
         for head in range(2):
             total = None
             for piece in range(4):
                 side, lane = piece // 2, (piece % 2) * 512
                 weight = qkv_all[pl.ds(head * members, members), :, pl.ds(piece * 512, 512)]
                 product = lax.dot_general(
-                    mixed_left[side, :, pl.ds(lane, 512)],
+                    halves[side][:, lane : lane + 512],
                     weight.reshape(members * weight.shape[1], 512),
                     NT,
                     preferred_element_type=F32,
@@ -326,17 +333,17 @@
         ]
         attended = jnp.concatenate(attended, axis=1)
         out_rows = members * 32
-        for lane in range(0, width, 512):
+        for lane in range(0, width, 1024):
             sides = []
             for start in (lane, width + lane):
                 product = jnp.dot(
                     attended,
-                    out_all[:, :, pl.ds(start, 512)].reshape(out_rows, 512),
+                    out_all[:, :, pl.ds(start, 1024)].reshape(out_rows, 1024),
                     preferred_element_type=F32,
                 )
-                sides.append(product.reshape(slices, 8, 512) * gate[:, pl.ds(start, 512)])
+                sides.append(product.reshape(slices, 8, 1024) * gate[:, pl.ds(start, 1024)])
             packed = jnp.concatenate(sides, axis=1)
-            partials[p, :, :, pl.ds(lane, 512)] = packed.astype(BF16)
+            partials[p, :, :, pl.ds(lane, 1024)] = packed.astype(BF16)
 
         @pl.when(is_last)
         def _():

time: 174 us -> 173 us (level)
  no operation moved by 1% of the time
where the time goes in v5:
time: 173 us; the launch traced here: 172 us
  Pallas kernels  169 us (98%)
  local copies, waits for them, and re-layouts  2.99 us (2%)
    pallas_call x1, Pallas kernels, local(): pl.pallas_call(functools.partial(kernel, (sections, slices, members, patc...  169 us

profile of v5, /device:TPU:4, one launch (start us, length us, event | category | flops | bytes accessed | tf_op | source)
XLA Modules:
  0.0 172.4 jit_solution(13837981028997167155)
XLA Ops:
  0.6 168.8 %shard_map.77 = (bf16[16,512]{1,0:T(8,128)(2,1)}, bf16[2,4,64,256]{3,2,1,0:T(8,128)(2,1)}) custom-call(bf16[4,16,1024]{2,1,0:T(8,128)(2,1)} %bitcast.25, f32[48,128]{1,0:T(8,128)} %bitcast.27, bf16[2,48,2048]{2,1,0:T(8,128)(2,1)} %bitcast.22, bf16[2,16,2048]{2,1,0:T(8,128)(2,1)} %bitcast.26, f32[2,128]{1,0:T(2,128)} %bitcast.29, bf16[2,4,64,256]{3,2,1,0:T(8,128)(2,1)} %bitcast.23), custom_call_target="tpu_custom_call" | custom-call | tf_op jit(solution)/shard_map/pallas_call | solution.py:521
  169.4 1.3 copy.11
  170.8 1.7 copy.12

commit v6 on v5

--- a/solution.py
+++ b/solution.py
@@ -306,8 +306,8 @@
         factor = math.log2(math.e) / math.sqrt(128)
         query = queries[p]
         summed, weight_sum = None, None
-        for first in range(0, members, 4):
-            blocks = [own_kv if n == 0 else caches.at[n] for n in range(first, first + 4)]
+        for first in range(0, members, 2):
+            blocks = [own_kv if n == 0 else caches.at[n] for n in range(first, first + 2)]
             scores = [
                 lax.dot_general(
                     query,

time: 173 us -> 174 us (level)
  no operation moved by 1% of the time
where the time goes in v6:
time: 174 us
  Pallas kernels  170 us (98%)
  local copies, waits for them, and re-layouts  2.99 us (2%)
    pallas_call x1, Pallas kernels, local(): pl.pallas_call(functools.partial(kernel, (sections, slices, members, patc...  170 us

profile of v6, /device:TPU:4, one launch (start us, length us, event | category | flops | bytes accessed | tf_op | source)
XLA Modules:
  0.0 173.7 jit_solution(8172508012300501331)
XLA Ops:
  0.6 170.0 %shard_map.77 = (bf16[16,512]{1,0:T(8,128)(2,1)}, bf16[2,4,64,256]{3,2,1,0:T(8,128)(2,1)}) custom-call(bf16[4,16,1024]{2,1,0:T(8,128)(2,1)} %bitcast.25, f32[48,128]{1,0:T(8,128)} %bitcast.27, bf16[2,48,2048]{2,1,0:T(8,128)(2,1)} %bitcast.22, bf16[2,16,2048]{2,1,0:T(8,128)(2,1)} %bitcast.26, f32[2,128]{1,0:T(2,128)} %bitcast.29, bf16[2,4,64,256]{3,2,1,0:T(8,128)(2,1)} %bitcast.23), custom_call_target="tpu_custom_call" | custom-call | tf_op jit(solution)/shard_map/pallas_call | solution.py:521
  170.7 1.3 copy.11
  172.0 1.7 copy.12
